TPU v7x, 256 devices: a whole 4x4x8 slice. The times are simulated.
256 devices in a mesh: row: 64 (over y, z, core), col: 4 (over x).
Axes of the slice: x: 4, y: 4, z: 8, core: 2. Of those that a mesh axis runs over, the one named last changes fastest.
Arguments:
- diag_block: float32 [1024, 1024], P('row', 'col'), may hold values from -3 to 3, as said below
- block_rhs: float32 [1024, 512], P('row', 'col'), may hold values from -6 to 6
- panel: float32 [262144, 1024], P('row', 'col'), may hold values from -0.1875 to 0.1875
- trailing_rhs: float32 [262144, 512], P('row', 'col'), may hold values from -6 to 6
Outputs:
- solved: float32 [1024, 512], P('row', 'col')
- trailing: float32 [262144, 512], P('row', 'col')
Inputs may be any that keep to these rules, and one draw needn't show every extreme that they name: diag_block is zero above its diagonal; its diagonal entries lie between 1.5 and 3.
All inputs are finite; a program needn't handle non-finite values.
Results may differ from a plain program's by a relative error of at most 0.000096.
Values sent between devices are 32-bit elements; how exact they have to be, the bound alone decides.
No kernel may reach another device: no remote copies, remote signals or barrier semaphores. Data moves between devices by JAX's collectives and lax.ppermute only.
A program may use at most 128 MiB of HBM per device.

v0:
```python
import functools

import jax
import jax.numpy as jnp
from jax import lax
from jax.experimental import pallas as pl
from jax.experimental.pallas import tpu as pltpu
from jax.sharding import PartitionSpec as P

NY, NZ, NC = 4, 8, 2
MIB = 1024 * 1024


def mm(a, b):
    return jnp.dot(a, b, preferred_element_type=jnp.float32, precision=lax.Precision.HIGHEST)


def tiny_inverses(blocks):
    n = len(blocks)
    lane = lax.broadcasted_iota(jnp.int32, (16, 128), 1)
    row = lax.broadcasted_iota(jnp.int32, (16, 128), 0)
    seg = lane // 16
    packed = []
    for a in blocks:
        p = jnp.zeros((16, 128), jnp.float32)
        for s in range(8):
            p = jnp.where(seg == s, a[16 * s : 16 * s + 16, :], p)
        packed.append(p)
    p = jnp.concatenate(packed, axis=0)
    lane_n = lax.broadcasted_iota(jnp.int32, (16 * n, 128), 1)
    r = jnp.where(lane == seg * 16 + row, 1.0, 0.0).astype(jnp.float32)
    r = jnp.broadcast_to(r[None], (n, 16, 128))
    row3 = lax.broadcasted_iota(jnp.int32, (n, 16, 128), 1)
    for j in range(16):
        idx = (lane_n // 16) * 16 + j
        column = jnp.take_along_axis(p, idx, axis=1).reshape(n, 16, 128)
        w = r[:, j : j + 1, :] / column[:, j : j + 1, :]
        r = jnp.where(row3 > j, r - column * w, jnp.where(row3 == j, w, r))
    return [
        jnp.concatenate([jnp.where(seg == s, r[b], 0.0) for s in range(8)], axis=0) for b in range(n)
    ]


def grow(a, d, s):
    i = lax.broadcasted_iota(jnp.int32, a.shape, 0)
    k = lax.broadcasted_iota(jnp.int32, a.shape, 1)
    off = (i // (2 * s) == k // (2 * s)) & ((i // s) % 2 == 1) & ((k // s) % 2 == 0)
    return d - mm(d, mm(jnp.where(off, a, 0.0), d))


BELOW = ((1, 0), (2, 0), (2, 1), (3, 0), (3, 1), (3, 2))


def split(a):
    high = a.astype(jnp.bfloat16)
    return high, (a - high.astype(jnp.float32)).astype(jnp.bfloat16)


def prepare_kernel(where, *refs):
    own4, other4, (inverse_out, start_out, mark, diagonal, rhs, inverse, start, sems) = refs[:4], refs[4:8], refs[8:]
    for refs4, core in ((own4, where[0]), (other4, 1 - where[0])):
        for n in range(NY):
            plane = (where[1] + n) % NY
            diagonal[plane, :, core] = refs4[n][:, :, :256]
            rhs[plane, :, core] = refs4[n][:, :, 256:]
    whole = [diagonal[k].reshape(256, 256) for k in range(NY)]
    blocks = []
    for k in range(NY):
        blocks += [whole[k][:128, :128], whole[k][128:, 128:]]
    ds = tiny_inverses(blocks)
    for s in (16, 32, 64):
        ds = [grow(a, d, s) for a, d in zip(blocks, ds)]
    lows = [mm(ds[2 * k + 1], mm(whole[k][128:, :128], ds[2 * k])) for k in range(NY)]
    for k in range(NY):
        inverse[k, :128, :128] = ds[2 * k]
        inverse[k, :128, 128:] = jnp.zeros((128, 128), jnp.float32)
        inverse[k, 128:, :128] = -lows[k]
        inverse[k, 128:, 128:] = ds[2 * k + 1]
    copies_out = [
        [pltpu.make_async_copy(inverse.at[k], inverse_out.at[k - 1], sems.at[0, k]) for k in range(1, NY)],
        [pltpu.make_async_copy(start.at[k], start_out.at[k], sems.at[1, k]) for k in range(NY)],
    ]
    for copy in copies_out[0]:
        copy.start()
    for k in range(NY):
        start[k] = mm(inverse[k], rhs[k].reshape(256, 512))
        copies_out[1][k].start()
    mark[...] = start[NY - 1, :8, :128]
    for copy in copies_out[0] + copies_out[1]:
        copy.wait()


def prepare(where, own, other):
    vmem = pl.BlockSpec(memory_space=pltpu.VMEM)
    return pl.pallas_call(
        prepare_kernel,
        out_shape=[pltpu.HBM(s, jnp.float32) for s in ((NY - 1, 256, 256), (NY, 256, 512))]
        + [jax.ShapeDtypeStruct((8, 128), jnp.float32)],
        in_specs=[pl.BlockSpec(memory_space=pltpu.SMEM)] + [vmem] * 8,
        out_specs=[pl.BlockSpec(memory_space=pltpu.HBM)] * 2 + [vmem],
        scratch_shapes=[
            pltpu.VMEM((NY, NZ, NC, 16, 256), jnp.float32),
            pltpu.VMEM((NY, NZ, NC, 16, 512), jnp.float32),
            pltpu.VMEM((NY, 256, 256), jnp.float32),
            pltpu.VMEM((NY, 256, 512), jnp.float32),
            pltpu.SemaphoreType.DMA((2, NY)),
        ],
        compiler_params=pltpu.CompilerParams(vmem_limit_bytes=16 * MIB),
        cost_estimate=pl.CostEstimate(flops=10 * 10**9, bytes_accessed=8 * MIB, transcendentals=0),
    )(where, *own, *other)


def solve_kernel(where, low_own, low_other, inverse_in, start_in, mark, own, right, far, left, *refs):
    stripe, *outs, x_ref, lower, inverse, start, panel, sems, panel_sems = refs
    core, col = where[0], where[4]
    fetches = [[pltpu.make_async_copy(start_in.at[k], start.at[k], sems.at[0, k])] for k in range(NY)]
    for k in range(1, NY):
        fetches[k].append(pltpu.make_async_copy(inverse_in.at[k - 1], inverse.at[k - 1], sems.at[1, k]))
    for copy in fetches[0] + fetches[1]:
        copy.start()
    for n in range(len(BELOW)):
        lower[n, :, core] = low_own[:, n]
        lower[n, :, 1 - core] = low_other[:, n]
    for copy in fetches[0]:
        copy.wait()
    for shift, piece in enumerate((own, right, far, left)):
        k = (col + shift) % 4
        pltpu.make_async_copy(piece, panel.at[k], panel_sems.at[k]).start()
    for copy in fetches[2] + fetches[3]:
        copy.start()
    for k in range(NY + 1):
        if 0 < k < NY:
            for copy in fetches[k]:
                copy.wait()
        if k > 0:
            pltpu.make_async_copy(own, panel.at[k - 1], panel_sems.at[k - 1]).wait()
        if k < NY:
            rows = slice(256 * k, 256 * k + 256)
            x = start[k]
            if k > 0:
                total = jnp.zeros((256, 512), jnp.float32)
                for j in range(k):
                    n = BELOW.index((k, j))
                    total += mm(lower[n].reshape(256, 256), x_ref[256 * j : 256 * j + 256, :])
                x = x - mm(inverse[k - 1], total)
            x_ref[rows, :] = x
        if k > 0:
            for t in range(panel.shape[1] // 256):
                tile = slice(256 * t, 256 * t + 256)
                ah, al = split(panel[k - 1, tile, :])
                part = jnp.dot(ah, xh, preferred_element_type=jnp.float32)
                part += jnp.dot(ah, xl, preferred_element_type=jnp.float32)
                part += jnp.dot(al, xh, preferred_element_type=jnp.float32)
                for j in range(4):
                    piece = part[:, 128 * j : 128 * j + 128]
                    outs[j][tile, :] = piece if k == 1 else outs[j][tile, :] + piece
        if k < NY:
            turned = [x_ref[rows, pl.ds(pl.multiple_of((col + j) % 4 * 128, 128), 128)] for j in range(4)]
            xh, xl = split(jnp.concatenate(turned, axis=1))
    stripe[...] = x_ref[pl.ds(pl.multiple_of(where[2], 16), 16), pl.ds(pl.multiple_of(where[3], 128), 128)]


def solve_and_multiply(where, low_own, low_other, inverse, start, mark, pieces):
    vmem, anywhere = pl.BlockSpec(memory_space=pltpu.VMEM), pl.BlockSpec(memory_space=pl.ANY)
    n = pieces[0].shape[0]
    return pl.pallas_call(
        solve_kernel,
        out_shape=[jax.ShapeDtypeStruct((16, 128), jnp.float32)] + [jax.ShapeDtypeStruct((n, 128), jnp.float32)] * 4,
        in_specs=[pl.BlockSpec(memory_space=pltpu.SMEM), vmem, vmem, anywhere, anywhere, vmem] + [anywhere] * 4,
        out_specs=[vmem] * 5,
        scratch_shapes=[
            pltpu.VMEM((1024, 512), jnp.float32),
            pltpu.VMEM((len(BELOW), NZ, NC, 16, 256), jnp.float32),
            pltpu.VMEM((NY - 1, 256, 256), jnp.float32),
            pltpu.VMEM((NY, 256, 512), jnp.float32),
            pltpu.VMEM((4, n, 256), jnp.float32),
            pltpu.SemaphoreType.DMA((2, NY)),
            pltpu.SemaphoreType.DMA((4,)),
        ],
        compiler_params=pltpu.CompilerParams(vmem_limit_bytes=20 * MIB),
        cost_estimate=pl.CostEstimate(flops=8 * 10**9, bytes_accessed=8 * MIB, transcendentals=0),
    )(where, low_own, low_other, inverse, start, mark, *pieces)


def finish_kernel(sources, rhs, *refs):
    pieces, out = refs[: sources.shape[0]], refs[-1]
    for n, piece in enumerate(pieces):

        @pl.when(pl.program_id(0) == n)
        def _():
            out[...] = rhs[...] - piece[...]


def finish(sources, rhs, pieces, before):
    block = pl.BlockSpec(pieces[0].shape, lambda i, s: (s[i], 0))
    prior = [] if before is None else [before]
    return pl.pallas_call(
        finish_kernel,
        out_shape=jax.ShapeDtypeStruct(rhs.shape, jnp.float32),
        grid_spec=pltpu.PrefetchScalarGridSpec(
            num_scalar_prefetch=1,
            grid=(len(pieces),),
            in_specs=[block]
            + [pl.BlockSpec(p.shape, lambda i, s: (0, 0)) for p in pieces]
            + [pl.BlockSpec(memory_space=pl.ANY)] * len(prior),
            out_specs=block,
        ),
        input_output_aliases={2 + len(pieces): 0} if prior else {},
        compiler_params=pltpu.CompilerParams(vmem_limit_bytes=16 * MIB),
        cost_estimate=pl.CostEstimate(flops=rhs.size, bytes_accessed=3 * rhs.size, transcendentals=0),
    )(sources, rhs, *pieces, *prior)


def copies_kernel(fill, n, *refs):
    out = refs[-1]
    fill(*refs)
    for i in range(1, n):
        out[i] = out[0]


def copies(fill, n, shape, *args):
    vmem = pl.BlockSpec(memory_space=pltpu.VMEM)
    inputs = pl.BlockSpec() if fill is fill_mine else vmem
    specs = [pl.BlockSpec(memory_space=pltpu.SMEM) if a.dtype == jnp.int32 else inputs for a in args]
    return pl.pallas_call(
        functools.partial(copies_kernel, fill, n),
        out_shape=jax.ShapeDtypeStruct((n,) + shape, jnp.float32),
        in_specs=specs,
        out_specs=vmem,
        compiler_params=pltpu.CompilerParams(vmem_limit_bytes=8 * MIB),
        cost_estimate=pl.CostEstimate(flops=0, bytes_accessed=MIB, transcendentals=0),
    )(*args)


def fill_mine(diag, rhs, out):
    out[0, :, :256] = diag[...]
    out[0, :, 256:] = rhs[...]


def fill_rest(where, mine, out):
    out[0, :, :256] = mine[where[1], :, :256]
    for c in range(4):
        out[0, :, 256 + 128 * c : 384 + 128 * c] = mine[c, :, 256:]


def fill_low(where, mine, *refs):
    out = refs[3]
    for n, (k, j) in enumerate(BELOW):
        step = (k - where[1] + NY) % NY
        part = mine[j, :, :256]
        for m in range(3):
            part = jnp.where(step == m + 1, refs[m][j], part)
        out[0, n] = part


def z_groups():
    return [[(y * NZ + z) * NC + c for z in range(NZ)] for y in range(NY) for c in range(NC)]


def y_groups():
    return [[(y * NZ + z) * NC + c for y in range(NY)] for z in range(NZ) for c in range(NC)]


def send_copies(a, axis, groups=None):
    return lax.all_to_all(a, axis, 0, 0, tiled=True, axis_index_groups=groups)


def swap_cores(a):
    return lax.ppermute(a, "row", [(i, i ^ 1) for i in range(NY * NZ * NC)])


def shift_y(a, k):
    step = k * NZ * NC
    n = NY * NZ * NC
    return lax.ppermute(a, "row", [(i, (i + step) % n) for i in range(n)])


def send_x(a, k):
    return lax.ppermute(a, "col", [(i, (i + k) % 4) for i in range(4)])


def per_device(diag_block, block_rhs, panel, trailing_rhs):
    row, col = lax.axis_index("row"), lax.axis_index("col")
    y = row // (NZ * NC)
    where = jnp.stack([row % NC, y, row * 16, col * 128, col]).astype(jnp.int32)

    mine = send_copies(copies(fill_mine, 4, (16, 384), *[pltpu.with_memory_space_constraint(a, pltpu.HBM) for a in (diag_block, block_rhs)]), "col")
    quarter = panel.shape[0] // 4
    own, *pieces = [lax.dynamic_slice_in_dim(panel, (col + k) % 4 * quarter, quarter, 0) for k in (0, 2, 1, 3)]
    mine, pieces = lax.optimization_barrier((mine, pieces))
    far, left, right = [send_x(p, k) for k, p in zip((2, 1, 3), pieces)]

    rest = send_copies(copies(fill_rest, NZ, (16, 768), where, mine), "row", z_groups())
    lows = [shift_y(mine[:3, :, :256], k) for k in (3, 2, 1)]
    rest, lows = lax.optimization_barrier((rest, lows))
    low = send_copies(copies(fill_low, NZ, (6, 16, 256), where, mine, *lows), "row", z_groups())
    rests = [rest] + [shift_y(rest, k) for k in (3, 2, 1)]
    swapped = [swap_cores(r) for r in rests]
    far, left, right, swapped[0] = lax.optimization_barrier((far, left, right, swapped[0]))
    inverse, start, mark = prepare(where, rests, swapped)
    low, mark = lax.optimization_barrier((low, mark))
    inverse, start = [pltpu.with_memory_space_constraint(a, pltpu.HBM) for a in (inverse, start)]
    stripe, mine, to_right, to_far, to_left = solve_and_multiply(
        where, low, swap_cores(low), inverse, start, mark, (own, right, far, left)
    )

    got_left, got_right, got_far = send_x(to_right, 1), send_x(to_left, 3), send_x(to_far, 2)

    def sources(*shifts):
        return jnp.stack([(col + k) % 4 for k in shifts]).astype(jnp.int32)

    trailing = finish(sources(0), trailing_rhs, [mine], None)
    trailing = finish(sources(3, 1), trailing_rhs, [got_left, got_right], trailing)
    trailing = finish(sources(2), trailing_rhs, [got_far], trailing)
    return (stripe, trailing)


def solution(mesh):
    specs = (P("row", "col"),) * 4
    return jax.shard_map(per_device, mesh=mesh, in_specs=specs, out_specs=(P("row", "col"),) * 2, check_vma=False)
```

profile of v0, /device:TPU:6, one launch (start us, length us, event | category | flops | bytes accessed | tf_op | source)
XLA Modules:
  0.0 113.3 jit_solution(18073654827674642780)
XLA Ops:
  0.6 1.4 %shard_map.59 = f32[4,16,384]{2,1,0:T(8,128)} custom-call(f32[16,256]{1,0:T(8,128)} %refs_0_.1, f32[16,128]{1,0:T(8,128)} %refs_1_.1), custom_call_target="tpu_custom_call" | custom-call | bytes 1048576 | tf_op jit(solution)/shard_map/pallas_call | solution.py:225
  2.0 5.5 %all-to-all-start = ((f32[4,16,384]{2,1,0:T(8,128)}), f32[4,16,384]{2,1,0:T(8,128)S(1)}, u32[]{:S(2)}, u32[]{:S(2)}) async-start(f32[4,16,384]{2,1,0:T(8,128)} %shard_map.59), calls=%async_computation | async-start | bytes 196608 | tf_op jit(solution)/shard_map/all_to_all | solution.py:265
  7.5 3.9 %constant_dynamic-slice_fusion = (f32[1024,256]{1,0:T(8,128)S(1)}, f32[1024,256]{1,0:T(8,128)}, f32[1024,256]{1,0:T(8,128)}, f32[1024,256]{1,0:T(8,128)}) fusion(f32[4096,256]{1,0:T(8,128)} %param.6, s32[]{:T(128)S(6)} %select_n.56, s32[]{:T(128)S(6)} %select_n.52, s32[]{:T(128)S(6)} %select_n.50, s32[]{:T(128)S(6)} %select_n.54), kind=kLoop, calls=%fused_computation | loop fusion | bytes 8388624 | tf_op jit(solution)/shard_map/dynamic_slice | solution.py:289
  11.4 1.9 %collective-permute-start.6 = (f32[1024,256]{1,0:T(8,128)}, f32[1024,256]{1,0:T(8,128)S(1)}, u32[]{:S(2)}, u32[]{:S(2)}) collective-permute-start(f32[1024,256]{1,0:T(8,128)} %get-tuple-element.29), channel_id=1, source_target_pairs={{0,2},{1,3},{2,0},{3,1},{4,6},{5,7},{6,4},{7,5},{8,10},{9,11},{10,... | collective-permute-start | bytes 3145736 | tf_op jit(solution)/shard_map/ppermute | solution.py:279
  13.4 1.3 %shard_map.60 = f32[8,16,768]{2,1,0:T(8,128)} custom-call(s32[5]{0:T(128)S(1)} %stack.38.refs_0_.where, f32[4,16,384]{2,1,0:T(8,128)S(1)} %all-to-all-done.refs_1_), custom_call_target="tpu_custom_call" | custom-call | bytes 1048576 | tf_op jit(solution)/shard_map/pallas_call | solution.py:225
  14.7 7.7 %all-to-all-start.1 = ((f32[8,16,768]{2,1,0:T(8,128)}), f32[8,16,768]{2,1,0:T(8,128)S(1)}, u32[]{:S(2)}, u32[]{:S(2)}) async-start(f32[8,16,768]{2,1,0:T(8,128)} %shard_map.60), calls=%async_computation.1 | async-start | bytes 786432 | tf_op jit(solution)/shard_map/all_to_all | solution.py:265
  22.5 1.7 %collective-permute-start.7 = (f32[1024,256]{1,0:T(8,128)}, f32[1024,256]{1,0:T(8,128)}, u32[]{:S(2)}, u32[]{:S(2)}) collective-permute-start(f32[1024,256]{1,0:T(8,128)} %get-tuple-element.30), channel_id=1, source_target_pairs={{0,1},{1,2},{2,3},{3,0},{4,5},{5,6},{6,7},{7,4},{8,9},{9,10},{10,1... | collective-permute-start | bytes 3145736 | tf_op jit(solution)/shard_map/ppermute | solution.py:279
  24.5 3.0 %collective-permute-start = (f32[3,16,256]{2,1,0:T(8,128)S(1)}, f32[3,16,256]{2,1,0:T(8,128)S(1)}, u32[]{:S(2)}, u32[]{:S(2)}) collective-permute-start(f32[3,16,256]{2,1,0:T(8,128)S(1)} %slice.2), channel_id=1, source_target_pairs={{0,192},{4,196},{8,200},{12,204},{16,208},{20,212},{24,216},{28,22... | collective-permute-start | bytes 147464 | tf_op jit(solution)/shard_map/ppermute | solution.py:275
  27.5 0.6 collective-permute-start.1
  28.1 1.1 collective-permute-done.refs_2_
  29.2 0.9 collective-permute-start.2
  30.2 3.0 %collective-permute-done.1.refs_3_ = f32[3,16,256]{2,1,0:T(8,128)S(1)} collective-permute-done((f32[3,16,256]{2,1,0:T(8,128)S(1)}, f32[3,16,256]{2,1,0:T(8,128)S(1)}, u32[]{:S(2)}, u32[]{:S(2)}) %collective-permute-start.1) | collective-permute-done | bytes 49184 | tf_op jit(solution)/shard_map/ppermute | solution.py:275
  33.2 1.7 %collective-permute-done.2.refs_4_ = f32[3,16,256]{2,1,0:T(8,128)S(1)} collective-permute-done((f32[3,16,256]{2,1,0:T(8,128)S(1)}, f32[3,16,256]{2,1,0:T(8,128)S(1)}, u32[]{:S(2)}, u32[]{:S(2)}) %collective-permute-start.2) | collective-permute-done | bytes 49184 | tf_op jit(solution)/shard_map/ppermute | solution.py:275
  34.9 1.0 all-to-all-done.1.refs_0_
  35.9 3.0 %collective-permute-start.3 = (f32[8,16,768]{2,1,0:T(8,128)S(1)}, f32[8,16,768]{2,1,0:T(8,128)}, u32[]{:S(2)}, u32[]{:S(2)}) collective-permute-start(f32[8,16,768]{2,1,0:T(8,128)S(1)} %all-to-all-done.1.refs_0_), channel_id=1, source_target_pairs={{0,192},{4,196},{8,200},{12,204},{16,208},{20,212},{24,216},{28,22... | collective-permute-start | bytes 1179656 | tf_op jit(solution)/shard_map/ppermute | solution.py:275
  39.6 1.0 collective-permute-start.5
  40.5 1.5 %shard_map.61 = f32[8,6,16,256]{3,2,1,0:T(8,128)} custom-call(s32[5]{0:T(128)S(1)} %stack.38.refs_0_.where, f32[4,16,384]{2,1,0:T(8,128)S(1)} %all-to-all-done.refs_1_, f32[3,16,256]{2,1,0:T(8,128)S(1)} %collective-permute-done.refs_2_, f32[3,16,256]{2,1,0:T(8,128)S(1)} %collective-permute-done.1.refs_3_, f32[3,16,256]{2,1,0:T(8,128)S(1)} %collective-permute-done.2.refs_4_), custom_call_target="tpu_custom_call" | custom-call | bytes 1048576 | tf_op jit(solution)/shard_map/pallas_call | solution.py:225
  42.0 8.1 %all-to-all-start.2 = ((f32[8,6,16,256]{3,2,1,0:T(8,128)}), f32[8,6,16,256]{3,2,1,0:T(8,128)S(1)}, u32[]{:S(2)}, u32[]{:S(2)}) async-start(f32[8,6,16,256]{3,2,1,0:T(8,128)} %shard_map.61), calls=%async_computation.2 | async-start | bytes 1572864 | tf_op jit(solution)/shard_map/all_to_all | solution.py:265
  50.1 7.6 %collective-permute-done.7.left = f32[1024,256]{1,0:T(8,128)} collective-permute-done((f32[1024,256]{1,0:T(8,128)}, f32[1024,256]{1,0:T(8,128)}, u32[]{:S(2)}, u32[]{:S(2)}) %collective-permute-start.7) | collective-permute-done | bytes 1048608 | tf_op jit(solution)/shard_map/ppermute | solution.py:279
  61.3 7.5 %shard_map.62 = (f32[3,256,256]{2,1,0:T(8,128)}, f32[4,256,512]{2,1,0:T(8,128)}, f32[8,128]{1,0:T(8,128)S(1)}) custom-call(s32[5]{0:T(128)S(1)} %stack.38.refs_0_.where, f32[8,16,768]{2,1,0:T(8,128)S(1)} %all-to-all-done.1.refs_0_, f32[8,16,768]{2,1,0:T(8,128)} %collective-permute-done.3.refs_1_, f32[8,16,768]{2,1,0:T(8,128)} %collective-permute-done.4.refs_2_, ...), custom_call_target="tpu_custom_call" | custom-call | flops 10000000000 | bytes 8388608 | tf_op jit(solution)/shard_map/pallas_call | solution.py:95
  68.9 0.9 all-to-all-done.2.low_own
  69.8 2.3 %collective-permute-done.13.low_other = f32[8,6,16,256]{3,2,1,0:T(8,128)S(1)} collective-permute-done((f32[8,6,16,256]{3,2,1,0:T(8,128)S(1)}, f32[8,6,16,256]{3,2,1,0:T(8,128)S(1)}, u32[]{:S(2)}, u32[]{:S(2)}) %collective-permute-start.13) | collective-permute-done | bytes 786464 | tf_op jit(solution)/shard_map/ppermute | solution.py:269
  72.1 12.1 %shard_map.63 = (f32[16,128]{1,0:T(8,128)}, f32[1024,128]{1,0:T(8,128)S(1)}, f32[1024,128]{1,0:T(8,128)S(1)}, f32[1024,128]{1,0:T(8,128)S(1)}, f32[1024,128]{1,0:T(8,128)S(1)}) custom-call(s32[5]{0:T(128)S(1)} %stack.38.refs_0_.where, f32[8,6,16,256]{3,2,1,0:T(8,128)S(1)} %all-to-all-done.2.low_own, f32[8,6,16,256]{3,2,1,0:T(8,128)S(1)} %collective-permute-done.13.low_other, ...), custom_call_target="tpu_custom_call" | custom-call | flops 8000000000 | bytes 8388608 | tf_op jit(solution)/shard_map/pallas_call | solution.py:166
  84.2 1.1 collective-permute-start.15
  85.3 1.0 collective-permute-start.16
  86.3 3.3 %collective-permute-start.14 = (f32[1024,128]{1,0:T(8,128)S(1)}, f32[1024,128]{1,0:T(8,128)S(1)}, u32[]{:S(2)}, u32[]{:S(2)}) collective-permute-start(f32[1024,128]{1,0:T(8,128)S(1)} %get-tuple-element.42), channel_id=1, source_target_pairs={{0,2},{1,3},{2,0},{3,1},{4,6},{5,7},{6,4},{7,5},{8,10},{9,11},{10,... | collective-permute-start | bytes 1572872 | tf_op jit(solution)/shard_map/ppermute | solution.py:279
  89.7 0.8 shard_map.64.refs_2_
  90.5 8.5 %collective-permute-done.15.refs_0_ = f32[1024,128]{1,0:T(8,128)S(1)} collective-permute-done((f32[1024,128]{1,0:T(8,128)S(1)}, f32[1024,128]{1,0:T(8,128)S(1)}, u32[]{:S(2)}, u32[]{:S(2)}) %collective-permute-start.15) | collective-permute-done | bytes 524320 | tf_op jit(solution)/shard_map/ppermute | solution.py:279
  99.0 1.2 %collective-permute-done.16.refs_1_ = f32[1024,128]{1,0:T(8,128)S(1)} collective-permute-done((f32[1024,128]{1,0:T(8,128)S(1)}, f32[1024,128]{1,0:T(8,128)S(1)}, u32[]{:S(2)}, u32[]{:S(2)}) %collective-permute-start.16) | collective-permute-done | bytes 524320 | tf_op jit(solution)/shard_map/ppermute | solution.py:279
  100.3 1.6 %shard_map.65.refs_1_ = f32[4096,128]{1,0:T(8,128)} custom-call(s32[2]{0:T(128)S(1)} %pad_add_fusion.sources, f32[4096,128]{1,0:T(8,128)S(1)} %copy-done, f32[1024,128]{1,0:T(8,128)S(1)} %collective-permute-done.15.refs_0_, f32[1024,128]{1,0:T(8,128)S(1)} %collective-permute-done.16.refs_1_, ...), custom_call_target="tpu_custom_call", output_to_operand_aliasing={{}: (4, {})} | custom-call | flops 524288 | bytes 1572864 | tf_op jit(solution)/shard_map/pallas_call | solution.py:197
  101.9 10.6 %collective-permute-done.14.refs_0_ = f32[1024,128]{1,0:T(8,128)S(1)} collective-permute-done((f32[1024,128]{1,0:T(8,128)S(1)}, f32[1024,128]{1,0:T(8,128)S(1)}, u32[]{:S(2)}, u32[]{:S(2)}) %collective-permute-start.14) | collective-permute-done | bytes 524320 | tf_op jit(solution)/shard_map/ppermute | solution.py:279
  112.5 0.8 shard_map.66
  (22 shorter events, 4.8 us)
Async XLA Ops:
  2.0 9.4 %all-to-all-start = ((f32[4,16,384]{2,1,0:T(8,128)}), f32[4,16,384]{2,1,0:T(8,128)S(1)}, u32[]{:S(2)}, u32[]{:S(2)}) async-start(f32[4,16,384]{2,1,0:T(8,128)} %shard_map.59), calls=%async_computation | async-start | bytes 196608 | tf_op jit(solution)/shard_map/all_to_all | solution.py:265
  11.4 28.1 %collective-permute-start.6 = (f32[1024,256]{1,0:T(8,128)}, f32[1024,256]{1,0:T(8,128)S(1)}, u32[]{:S(2)}, u32[]{:S(2)}) collective-permute-start(f32[1024,256]{1,0:T(8,128)} %get-tuple-element.29), channel_id=1, source_target_pairs={{0,2},{1,3},{2,0},{3,1},{4,6},{5,7},{6,4},{7,5},{8,10},{9,11},{10,... | collective-permute-start | bytes 3145736 | tf_op jit(solution)/shard_map/ppermute | solution.py:279
  14.7 21.2 %all-to-all-start.1 = ((f32[8,16,768]{2,1,0:T(8,128)}), f32[8,16,768]{2,1,0:T(8,128)S(1)}, u32[]{:S(2)}, u32[]{:S(2)}) async-start(f32[8,16,768]{2,1,0:T(8,128)} %shard_map.60), calls=%async_computation.1 | async-start | bytes 786432 | tf_op jit(solution)/shard_map/all_to_all | solution.py:265
  22.5 35.3 %collective-permute-start.7 = (f32[1024,256]{1,0:T(8,128)}, f32[1024,256]{1,0:T(8,128)}, u32[]{:S(2)}, u32[]{:S(2)}) collective-permute-start(f32[1024,256]{1,0:T(8,128)} %get-tuple-element.30), channel_id=1, source_target_pairs={{0,1},{1,2},{2,3},{3,0},{4,5},{5,6},{6,7},{7,4},{8,9},{9,10},{10,1... | collective-permute-start | bytes 3145736 | tf_op jit(solution)/shard_map/ppermute | solution.py:279
  24.1 35.2 %collective-permute-start.8 = (f32[1024,256]{1,0:T(8,128)}, f32[1024,256]{1,0:T(8,128)}, u32[]{:S(2)}, u32[]{:S(2)}) collective-permute-start(f32[1024,256]{1,0:T(8,128)} %get-tuple-element.31), channel_id=1, source_target_pairs={{0,3},{1,0},{2,1},{3,2},{4,7},{5,4},{6,5},{7,6},{8,11},{9,8},{10,9... | collective-permute-start | bytes 3145736 | tf_op jit(solution)/shard_map/ppermute | solution.py:279
  24.5 4.8 %collective-permute-start = (f32[3,16,256]{2,1,0:T(8,128)S(1)}, f32[3,16,256]{2,1,0:T(8,128)S(1)}, u32[]{:S(2)}, u32[]{:S(2)}) collective-permute-start(f32[3,16,256]{2,1,0:T(8,128)S(1)} %slice.2), channel_id=1, source_target_pairs={{0,192},{4,196},{8,200},{12,204},{16,208},{20,212},{24,216},{28,22... | collective-permute-start | bytes 147464 | tf_op jit(solution)/shard_map/ppermute | solution.py:275
  27.5 5.7 %collective-permute-start.1 = (f32[3,16,256]{2,1,0:T(8,128)S(1)}, f32[3,16,256]{2,1,0:T(8,128)S(1)}, u32[]{:S(2)}, u32[]{:S(2)}) collective-permute-start(f32[3,16,256]{2,1,0:T(8,128)S(1)} %slice.2), channel_id=1, source_target_pairs={{0,128},{4,132},{8,136},{12,140},{16,144},{20,148},{24,152},{28,15... | collective-permute-start | bytes 147464 | tf_op jit(solution)/shard_map/ppermute | solution.py:275
  29.2 5.6 %collective-permute-start.2 = (f32[3,16,256]{2,1,0:T(8,128)S(1)}, f32[3,16,256]{2,1,0:T(8,128)S(1)}, u32[]{:S(2)}, u32[]{:S(2)}) collective-permute-start(f32[3,16,256]{2,1,0:T(8,128)S(1)} %slice.2), channel_id=1, source_target_pairs={{0,64},{4,68},{8,72},{12,76},{16,80},{20,84},{24,88},{28,92},{32,9... | collective-permute-start | bytes 147464 | tf_op jit(solution)/shard_map/ppermute | solution.py:275
  35.9 21.8 %collective-permute-start.3 = (f32[8,16,768]{2,1,0:T(8,128)S(1)}, f32[8,16,768]{2,1,0:T(8,128)}, u32[]{:S(2)}, u32[]{:S(2)}) collective-permute-start(f32[8,16,768]{2,1,0:T(8,128)S(1)} %all-to-all-done.1.refs_0_), channel_id=1, source_target_pairs={{0,192},{4,196},{8,200},{12,204},{16,208},{20,212},{24,216},{28,22... | collective-permute-start | bytes 1179656 | tf_op jit(solution)/shard_map/ppermute | solution.py:275
  38.9 19.3 %collective-permute-start.4 = (f32[8,16,768]{2,1,0:T(8,128)S(1)}, f32[8,16,768]{2,1,0:T(8,128)}, u32[]{:S(2)}, u32[]{:S(2)}) collective-permute-start(f32[8,16,768]{2,1,0:T(8,128)S(1)} %all-to-all-done.1.refs_0_), channel_id=1, source_target_pairs={{0,128},{4,132},{8,136},{12,140},{16,144},{20,148},{24,152},{28,15... | collective-permute-start | bytes 1179656 | tf_op jit(solution)/shard_map/ppermute | solution.py:275
  39.6 18.8 %collective-permute-start.5 = (f32[8,16,768]{2,1,0:T(8,128)S(1)}, f32[8,16,768]{2,1,0:T(8,128)}, u32[]{:S(2)}, u32[]{:S(2)}) collective-permute-start(f32[8,16,768]{2,1,0:T(8,128)S(1)} %all-to-all-done.1.refs_0_), channel_id=1, source_target_pairs={{0,64},{4,68},{8,72},{12,76},{16,80},{20,84},{24,88},{28,92},{32,9... | collective-permute-start | bytes 1179656 | tf_op jit(solution)/shard_map/ppermute | solution.py:275
  42.0 27.7 %all-to-all-start.2 = ((f32[8,6,16,256]{3,2,1,0:T(8,128)}), f32[8,6,16,256]{3,2,1,0:T(8,128)S(1)}, u32[]{:S(2)}, u32[]{:S(2)}) async-start(f32[8,6,16,256]{3,2,1,0:T(8,128)} %shard_map.61), calls=%async_computation.2 | async-start | bytes 1572864 | tf_op jit(solution)/shard_map/all_to_all | solution.py:265
  57.7 2.2 %collective-permute-start.9 = (f32[8,16,768]{2,1,0:T(8,128)S(1)}, f32[8,16,768]{2,1,0:T(8,128)S(1)}, u32[]{:S(2)}, u32[]{:S(2)}) collective-permute-start(f32[8,16,768]{2,1,0:T(8,128)S(1)} %all-to-all-done.1.refs_0_), channel_id=1, source_target_pairs={{0,4},{4,0},{8,12},{12,8},{16,20},{20,16},{24,28},{28,24},{32,36},... | collective-permute-start | bytes 1179656 | tf_op jit(solution)/shard_map/ppermute | solution.py:269
  57.7 2.5 %collective-permute-start.10 = (f32[8,16,768]{2,1,0:T(8,128)}, f32[8,16,768]{2,1,0:T(8,128)S(1)}, u32[]{:S(2)}, u32[]{:S(2)}) collective-permute-start(f32[8,16,768]{2,1,0:T(8,128)} %collective-permute-done.3.refs_1_), channel_id=1, source_target_pairs={{0,4},{4,0},{8,12},{12,8},{16,20},{20,16},{24,28},{28,24},{32,36},... | collective-permute-start | bytes 1179656 | tf_op jit(solution)/shard_map/ppermute | solution.py:269
  58.2 2.5 %collective-permute-start.11 = (f32[8,16,768]{2,1,0:T(8,128)}, f32[8,16,768]{2,1,0:T(8,128)S(1)}, u32[]{:S(2)}, u32[]{:S(2)}) collective-permute-start(f32[8,16,768]{2,1,0:T(8,128)} %collective-permute-done.4.refs_2_), channel_id=1, source_target_pairs={{0,4},{4,0},{8,12},{12,8},{16,20},{20,16},{24,28},{28,24},{32,36},... | collective-permute-start | bytes 1179656 | tf_op jit(solution)/shard_map/ppermute | solution.py:269
  58.3 3.0 %collective-permute-start.12 = (f32[8,16,768]{2,1,0:T(8,128)}, f32[8,16,768]{2,1,0:T(8,128)S(1)}, u32[]{:S(2)}, u32[]{:S(2)}) collective-permute-start(f32[8,16,768]{2,1,0:T(8,128)} %collective-permute-done.5.refs_3_), channel_id=1, source_target_pairs={{0,4},{4,0},{8,12},{12,8},{16,20},{20,16},{24,28},{28,24},{32,36},... | collective-permute-start | bytes 1179656 | tf_op jit(solution)/shard_map/ppermute | solution.py:269
  69.8 2.3 %collective-permute-start.13 = (f32[8,6,16,256]{3,2,1,0:T(8,128)S(1)}, f32[8,6,16,256]{3,2,1,0:T(8,128)S(1)}, u32[]{:S(2)}, u32[]{:S(2)}) collective-permute-start(f32[8,6,16,256]{3,2,1,0:T(8,128)S(1)} %all-to-all-done.2.low_own), channel_id=1, source_target_pairs={{0,4},{4,0},{8,12},{12,8},{16,20},{20,16},{24,28},{28,24},{32,36},... | collective-permute-start | bytes 2359304 | tf_op jit(solution)/shard_map/ppermute | solution.py:269
  72.0 17.6 %copy-start = (f32[4096,128]{1,0:T(8,128)S(1)}, f32[4096,128]{1,0:T(8,128)}, u32[]{:S(2)}) copy-start(f32[4096,128]{1,0:T(8,128)} %rhs.5) | copy-start | bytes 6291460
  84.2 14.9 %collective-permute-start.15 = (f32[1024,128]{1,0:T(8,128)S(1)}, f32[1024,128]{1,0:T(8,128)S(1)}, u32[]{:S(2)}, u32[]{:S(2)}) collective-permute-start(f32[1024,128]{1,0:T(8,128)S(1)} %get-tuple-element.43), channel_id=1, source_target_pairs={{0,1},{1,2},{2,3},{3,0},{4,5},{5,6},{6,7},{7,4},{8,9},{9,10},{10,1... | collective-permute-start | bytes 1572872 | tf_op jit(solution)/shard_map/ppermute | solution.py:279
  85.3 15.0 %collective-permute-start.16 = (f32[1024,128]{1,0:T(8,128)S(1)}, f32[1024,128]{1,0:T(8,128)S(1)}, u32[]{:S(2)}, u32[]{:S(2)}) collective-permute-start(f32[1024,128]{1,0:T(8,128)S(1)} %get-tuple-element.44), channel_id=1, source_target_pairs={{0,3},{1,0},{2,1},{3,2},{4,7},{5,4},{6,5},{7,6},{8,11},{9,8},{10,9... | collective-permute-start | bytes 1572872 | tf_op jit(solution)/shard_map/ppermute | solution.py:279
  86.3 26.2 %collective-permute-start.14 = (f32[1024,128]{1,0:T(8,128)S(1)}, f32[1024,128]{1,0:T(8,128)S(1)}, u32[]{:S(2)}, u32[]{:S(2)}) collective-permute-start(f32[1024,128]{1,0:T(8,128)S(1)} %get-tuple-element.42), channel_id=1, source_target_pairs={{0,2},{1,3},{2,0},{3,1},{4,6},{5,7},{6,4},{7,5},{8,10},{9,11},{10,... | collective-permute-start | bytes 1572872 | tf_op jit(solution)/shard_map/ppermute | solution.py:279
where the time goes:
time: 114 us; the launch traced here: 113 us
  starting transfers between devices  40.8 us (36%)
  waiting for transfers between devices  40.6 us (36%)
  Pallas kernels  27.1 us (24%)
  local copies, waits for them, and re-layouts  4.04 us (4%)
    ppermute x6, waiting for transfers between devices, send_x(): return lax.ppermute(a, 'col', [(i, (i + k) % 4) for i in range(4)])  28.6 us
    all_to_all x3, starting transfers between devices, send_copies(): return lax.all_to_all(a, axis, 0, 0, tiled=True, axis_index_groups=groups)  21.3 us
    pallas_call x1, Pallas kernels, solve_and_multiply(): pl.pallas_call(solve_kernel, out_shape=[jax.ShapeDtypeStruct((16, 128), j...  12.1 us
    ppermute x6, starting transfers between devices, send_x(): return lax.ppermute(a, 'col', [(i, (i + k) % 4) for i in range(4)])  9.3 us
    ppermute x6, starting transfers between devices, shift_y(): return lax.ppermute(a, 'row', [(i, (i + step) % n) for i in range(n)])  9.16 us
    pallas_call x1, Pallas kernels, prepare(): pl.pallas_call(prepare_kernel, out_shape=[pltpu.HBM(s, jnp.float32) for s...  7.51 us
    ppermute x6, waiting for transfers between devices, shift_y(): return lax.ppermute(a, 'row', [(i, (i + step) % n) for i in range(n)])  5.84 us
    ppermute x5, waiting for transfers between devices, swap_cores(): return lax.ppermute(a, 'row', [(i, i ^ 1) for i in range(NY * NZ * NC)])  4.25 us
  transfers between devices with their start and end apart: 20, of which 15 were waited for; matrix products, arithmetic and copies ran while one was open for 4% of the time, Pallas kernels for 11%

commit v1 on v0

--- a/solution.py
+++ b/solution.py
@@ -110,6 +110,9 @@
     )(where, *own, *other)
 
 
+TAKE = ((), (), (), (0, 1, 2), (3,))
+
+
 def solve_kernel(where, low_own, low_other, inverse_in, start_in, mark, own, right, far, left, *refs):
     stripe, *outs, x_ref, lower, inverse, start, panel, sems, panel_sems = refs
     core, col = where[0], where[4]
@@ -128,12 +131,13 @@
         pltpu.make_async_copy(piece, panel.at[k], panel_sems.at[k]).start()
     for copy in fetches[2] + fetches[3]:
         copy.start()
+    halves = []
     for k in range(NY + 1):
         if 0 < k < NY:
             for copy in fetches[k]:
                 copy.wait()
-        if k > 0:
-            pltpu.make_async_copy(own, panel.at[k - 1], panel_sems.at[k - 1]).wait()
+        for j in TAKE[k]:
+            pltpu.make_async_copy(own, panel.at[j], panel_sems.at[j]).wait()
         if k < NY:
             rows = slice(256 * k, 256 * k + 256)
             x = start[k]
@@ -144,19 +148,20 @@
                     total += mm(lower[n].reshape(256, 256), x_ref[256 * j : 256 * j + 256, :])
                 x = x - mm(inverse[k - 1], total)
             x_ref[rows, :] = x
-        if k > 0:
+        if TAKE[k]:
+            high, low = [jnp.concatenate([x[n] for x in halves[TAKE[k][0] :]], axis=0) for n in range(2)]
             for t in range(panel.shape[1] // 256):
                 tile = slice(256 * t, 256 * t + 256)
-                ah, al = split(panel[k - 1, tile, :])
-                part = jnp.dot(ah, xh, preferred_element_type=jnp.float32)
-                part += jnp.dot(ah, xl, preferred_element_type=jnp.float32)
-                part += jnp.dot(al, xh, preferred_element_type=jnp.float32)
+                ah, al = split(jnp.concatenate([panel[j, tile, :] for j in TAKE[k]], axis=1))
+                part = jnp.dot(ah, high, preferred_element_type=jnp.float32)
+                part += jnp.dot(ah, low, preferred_element_type=jnp.float32)
+                part += jnp.dot(al, high, preferred_element_type=jnp.float32)
                 for j in range(4):
                     piece = part[:, 128 * j : 128 * j + 128]
-                    outs[j][tile, :] = piece if k == 1 else outs[j][tile, :] + piece
+                    outs[j][tile, :] = piece if TAKE[k][0] == 0 else outs[j][tile, :] + piece
         if k < NY:
             turned = [x_ref[rows, pl.ds(pl.multiple_of((col + j) % 4 * 128, 128), 128)] for j in range(4)]
-            xh, xl = split(jnp.concatenate(turned, axis=1))
+            halves.append(split(jnp.concatenate(turned, axis=1)))
     stripe[...] = x_ref[pl.ds(pl.multiple_of(where[2], 16), 16), pl.ds(pl.multiple_of(where[3], 128), 128)]
 
 

time: 114 us -> 114 us (level)
  waiting for transfers between devices: 40.6 us -> 42.9 us
    ppermute x6, waiting for transfers between devices: 28.6 us -> 30.9 us  [send_x(): return lax.ppermute(a, 'col', [(i, (i + k) % 4) for i in range(4)])]
  transfers between devices with their start and end apart: 20 -> 20, of which waited for: 15 -> 14; matrix products, arithmetic and copies ran while one was open for 4% -> 4% of each run, Pallas kernels for 11% -> 11%
where the time goes in v1:
time: 114 us
  waiting for transfers between devices  42.9 us (38%)
  starting transfers between devices  40.1 us (35%)
  Pallas kernels  26.2 us (23%)
  local copies, waits for them, and re-layouts  4.04 us (4%)
    ppermute x6, waiting for transfers between devices, send_x(): return lax.ppermute(a, 'col', [(i, (i + k) % 4) for i in range(4)])  30.9 us
    all_to_all x3, starting transfers between devices, send_copies(): return lax.all_to_all(a, axis, 0, 0, tiled=True, axis_index_groups=groups)  21.3 us
    pallas_call x1, Pallas kernels, solve_and_multiply(): pl.pallas_call(solve_kernel, out_shape=[jax.ShapeDtypeStruct((16, 128), j...  11.2 us
    ppermute x6, starting transfers between devices, shift_y(): return lax.ppermute(a, 'row', [(i, (i + step) % n) for i in range(n)])  9.16 us
    ppermute x6, starting transfers between devices, send_x(): return lax.ppermute(a, 'col', [(i, (i + k) % 4) for i in range(4)])  8.53 us
    pallas_call x1, Pallas kernels, prepare(): pl.pallas_call(prepare_kernel, out_shape=[pltpu.HBM(s, jnp.float32) for s...  7.51 us
    ppermute x6, waiting for transfers between devices, shift_y(): return lax.ppermute(a, 'row', [(i, (i + step) % n) for i in range(n)])  5.84 us
    ppermute x5, waiting for transfers between devices, swap_cores(): return lax.ppermute(a, 'row', [(i, i ^ 1) for i in range(NY * NZ * NC)])  4.25 us
  transfers between devices with their start and end apart: 20, of which 14 were waited for; matrix products, arithmetic and copies ran while one was open for 4% of the time, Pallas kernels for 11%

profile of v1, /device:TPU:6, one launch (start us, length us, event | category | flops | bytes accessed | tf_op | source)
XLA Modules:
  0.0 113.9 jit_solution(4954055391175335231)
XLA Ops:
  0.6 1.4 %shard_map.59 = f32[4,16,384]{2,1,0:T(8,128)} custom-call(f32[16,256]{1,0:T(8,128)} %refs_0_.1, f32[16,128]{1,0:T(8,128)} %refs_1_.1), custom_call_target="tpu_custom_call" | custom-call | bytes 1048576 | tf_op jit(solution)/shard_map/pallas_call | solution.py:230
  2.0 5.5 %all-to-all-start = ((f32[4,16,384]{2,1,0:T(8,128)}), f32[4,16,384]{2,1,0:T(8,128)S(1)}, u32[]{:S(2)}, u32[]{:S(2)}) async-start(f32[4,16,384]{2,1,0:T(8,128)} %shard_map.59), calls=%async_computation | async-start | bytes 196608 | tf_op jit(solution)/shard_map/all_to_all | solution.py:270
  7.5 3.9 %constant_dynamic-slice_fusion = (f32[1024,256]{1,0:T(8,128)S(1)}, f32[1024,256]{1,0:T(8,128)}, f32[1024,256]{1,0:T(8,128)}, f32[1024,256]{1,0:T(8,128)}) fusion(f32[4096,256]{1,0:T(8,128)} %param.6, s32[]{:T(128)S(6)} %select_n.56, s32[]{:T(128)S(6)} %select_n.52, s32[]{:T(128)S(6)} %select_n.50, s32[]{:T(128)S(6)} %select_n.54), kind=kLoop, calls=%fused_computation | loop fusion | bytes 8388624 | tf_op jit(solution)/shard_map/dynamic_slice | solution.py:294
  11.4 1.9 %collective-permute-start.6 = (f32[1024,256]{1,0:T(8,128)}, f32[1024,256]{1,0:T(8,128)S(1)}, u32[]{:S(2)}, u32[]{:S(2)}) collective-permute-start(f32[1024,256]{1,0:T(8,128)} %get-tuple-element.29), channel_id=1, source_target_pairs={{0,2},{1,3},{2,0},{3,1},{4,6},{5,7},{6,4},{7,5},{8,10},{9,11},{10,... | collective-permute-start | bytes 3145736 | tf_op jit(solution)/shard_map/ppermute | solution.py:284
  13.4 1.3 %shard_map.60 = f32[8,16,768]{2,1,0:T(8,128)} custom-call(s32[5]{0:T(128)S(1)} %stack.38.refs_0_.where, f32[4,16,384]{2,1,0:T(8,128)S(1)} %all-to-all-done.refs_1_), custom_call_target="tpu_custom_call" | custom-call | bytes 1048576 | tf_op jit(solution)/shard_map/pallas_call | solution.py:230
  14.7 7.7 %all-to-all-start.1 = ((f32[8,16,768]{2,1,0:T(8,128)}), f32[8,16,768]{2,1,0:T(8,128)S(1)}, u32[]{:S(2)}, u32[]{:S(2)}) async-start(f32[8,16,768]{2,1,0:T(8,128)} %shard_map.60), calls=%async_computation.1 | async-start | bytes 786432 | tf_op jit(solution)/shard_map/all_to_all | solution.py:270
  22.5 1.7 %collective-permute-start.7 = (f32[1024,256]{1,0:T(8,128)}, f32[1024,256]{1,0:T(8,128)}, u32[]{:S(2)}, u32[]{:S(2)}) collective-permute-start(f32[1024,256]{1,0:T(8,128)} %get-tuple-element.30), channel_id=1, source_target_pairs={{0,1},{1,2},{2,3},{3,0},{4,5},{5,6},{6,7},{7,4},{8,9},{9,10},{10,1... | collective-permute-start | bytes 3145736 | tf_op jit(solution)/shard_map/ppermute | solution.py:284
  24.5 3.0 %collective-permute-start = (f32[3,16,256]{2,1,0:T(8,128)S(1)}, f32[3,16,256]{2,1,0:T(8,128)S(1)}, u32[]{:S(2)}, u32[]{:S(2)}) collective-permute-start(f32[3,16,256]{2,1,0:T(8,128)S(1)} %slice.2), channel_id=1, source_target_pairs={{0,192},{4,196},{8,200},{12,204},{16,208},{20,212},{24,216},{28,22... | collective-permute-start | bytes 147464 | tf_op jit(solution)/shard_map/ppermute | solution.py:280
  27.5 0.6 collective-permute-start.1
  28.1 1.1 collective-permute-done.refs_2_
  29.2 0.9 collective-permute-start.2
  30.2 3.0 %collective-permute-done.1.refs_3_ = f32[3,16,256]{2,1,0:T(8,128)S(1)} collective-permute-done((f32[3,16,256]{2,1,0:T(8,128)S(1)}, f32[3,16,256]{2,1,0:T(8,128)S(1)}, u32[]{:S(2)}, u32[]{:S(2)}) %collective-permute-start.1) | collective-permute-done | bytes 49184 | tf_op jit(solution)/shard_map/ppermute | solution.py:280
  33.2 1.7 %collective-permute-done.2.refs_4_ = f32[3,16,256]{2,1,0:T(8,128)S(1)} collective-permute-done((f32[3,16,256]{2,1,0:T(8,128)S(1)}, f32[3,16,256]{2,1,0:T(8,128)S(1)}, u32[]{:S(2)}, u32[]{:S(2)}) %collective-permute-start.2) | collective-permute-done | bytes 49184 | tf_op jit(solution)/shard_map/ppermute | solution.py:280
  34.9 1.0 all-to-all-done.1.refs_0_
  35.9 3.0 %collective-permute-start.3 = (f32[8,16,768]{2,1,0:T(8,128)S(1)}, f32[8,16,768]{2,1,0:T(8,128)}, u32[]{:S(2)}, u32[]{:S(2)}) collective-permute-start(f32[8,16,768]{2,1,0:T(8,128)S(1)} %all-to-all-done.1.refs_0_), channel_id=1, source_target_pairs={{0,192},{4,196},{8,200},{12,204},{16,208},{20,212},{24,216},{28,22... | collective-permute-start | bytes 1179656 | tf_op jit(solution)/shard_map/ppermute | solution.py:280
  38.9 0.6 collective-permute-start.4
  39.6 1.0 collective-permute-start.5
  40.5 1.5 %shard_map.61 = f32[8,6,16,256]{3,2,1,0:T(8,128)} custom-call(s32[5]{0:T(128)S(1)} %stack.38.refs_0_.where, f32[4,16,384]{2,1,0:T(8,128)S(1)} %all-to-all-done.refs_1_, f32[3,16,256]{2,1,0:T(8,128)S(1)} %collective-permute-done.refs_2_, f32[3,16,256]{2,1,0:T(8,128)S(1)} %collective-permute-done.1.refs_3_, f32[3,16,256]{2,1,0:T(8,128)S(1)} %collective-permute-done.2.refs_4_), custom_call_target="tpu_custom_call" | custom-call | bytes 1048576 | tf_op jit(solution)/shard_map/pallas_call | solution.py:230
  42.0 8.1 %all-to-all-start.2 = ((f32[8,6,16,256]{3,2,1,0:T(8,128)}), f32[8,6,16,256]{3,2,1,0:T(8,128)S(1)}, u32[]{:S(2)}, u32[]{:S(2)}) async-start(f32[8,6,16,256]{3,2,1,0:T(8,128)} %shard_map.61), calls=%async_computation.2 | async-start | bytes 1572864 | tf_op jit(solution)/shard_map/all_to_all | solution.py:270
  50.1 7.6 %collective-permute-done.7.left = f32[1024,256]{1,0:T(8,128)} collective-permute-done((f32[1024,256]{1,0:T(8,128)}, f32[1024,256]{1,0:T(8,128)}, u32[]{:S(2)}, u32[]{:S(2)}) %collective-permute-start.7) | collective-permute-done | bytes 1048608 | tf_op jit(solution)/shard_map/ppermute | solution.py:284
  58.7 0.6 collective-permute-done.8.right
  61.3 7.5 %shard_map.62 = (f32[3,256,256]{2,1,0:T(8,128)}, f32[4,256,512]{2,1,0:T(8,128)}, f32[8,128]{1,0:T(8,128)S(1)}) custom-call(s32[5]{0:T(128)S(1)} %stack.38.refs_0_.where, f32[8,16,768]{2,1,0:T(8,128)S(1)} %all-to-all-done.1.refs_0_, f32[8,16,768]{2,1,0:T(8,128)} %collective-permute-done.3.refs_1_, f32[8,16,768]{2,1,0:T(8,128)} %collective-permute-done.4.refs_2_, ...), custom_call_target="tpu_custom_call" | custom-call | flops 10000000000 | bytes 8388608 | tf_op jit(solution)/shard_map/pallas_call | solution.py:95
  68.9 0.9 all-to-all-done.2.low_own
  69.8 2.3 %collective-permute-done.13.low_other = f32[8,6,16,256]{3,2,1,0:T(8,128)S(1)} collective-permute-done((f32[8,6,16,256]{3,2,1,0:T(8,128)S(1)}, f32[8,6,16,256]{3,2,1,0:T(8,128)S(1)}, u32[]{:S(2)}, u32[]{:S(2)}) %collective-permute-start.13) | collective-permute-done | bytes 786464 | tf_op jit(solution)/shard_map/ppermute | solution.py:274
  72.1 11.2 %shard_map.63 = (f32[16,128]{1,0:T(8,128)}, f32[1024,128]{1,0:T(8,128)S(1)}, f32[1024,128]{1,0:T(8,128)S(1)}, f32[1024,128]{1,0:T(8,128)S(1)}, f32[1024,128]{1,0:T(8,128)S(1)}) custom-call(s32[5]{0:T(128)S(1)} %stack.38.refs_0_.where, f32[8,6,16,256]{3,2,1,0:T(8,128)S(1)} %all-to-all-done.2.low_own, f32[8,6,16,256]{3,2,1,0:T(8,128)S(1)} %collective-permute-done.13.low_other, ...), custom_call_target="tpu_custom_call" | custom-call | flops 8000000000 | bytes 8388608 | tf_op jit(solution)/shard_map/pallas_call | solution.py:171
  83.2 2.1 %collective-permute-start.15 = (f32[1024,128]{1,0:T(8,128)S(1)}, f32[1024,128]{1,0:T(8,128)S(1)}, u32[]{:S(2)}, u32[]{:S(2)}) collective-permute-start(f32[1024,128]{1,0:T(8,128)S(1)} %get-tuple-element.43), channel_id=1, source_target_pairs={{0,1},{1,2},{2,3},{3,0},{4,5},{5,6},{6,7},{7,4},{8,9},{9,10},{10,1... | collective-permute-start | bytes 1572872 | tf_op jit(solution)/shard_map/ppermute | solution.py:284
  85.3 2.5 %collective-permute-start.14 = (f32[1024,128]{1,0:T(8,128)S(1)}, f32[1024,128]{1,0:T(8,128)S(1)}, u32[]{:S(2)}, u32[]{:S(2)}) collective-permute-start(f32[1024,128]{1,0:T(8,128)S(1)} %get-tuple-element.42), channel_id=1, source_target_pairs={{0,2},{1,3},{2,0},{3,1},{4,6},{5,7},{6,4},{7,5},{8,10},{9,11},{10,... | collective-permute-start | bytes 1572872 | tf_op jit(solution)/shard_map/ppermute | solution.py:284
  87.9 0.8 shard_map.64.refs_2_
  88.8 19.3 %collective-permute-done.15.refs_0_ = f32[1024,128]{1,0:T(8,128)S(1)} collective-permute-done((f32[1024,128]{1,0:T(8,128)S(1)}, f32[1024,128]{1,0:T(8,128)S(1)}, u32[]{:S(2)}, u32[]{:S(2)}) %collective-permute-start.15) | collective-permute-done | bytes 524320 | tf_op jit(solution)/shard_map/ppermute | solution.py:284
  108.1 3.4 %collective-permute-done.16.refs_1_ = f32[1024,128]{1,0:T(8,128)S(1)} collective-permute-done((f32[1024,128]{1,0:T(8,128)S(1)}, f32[1024,128]{1,0:T(8,128)S(1)}, u32[]{:S(2)}, u32[]{:S(2)}) %collective-permute-start.16) | collective-permute-done | bytes 524320 | tf_op jit(solution)/shard_map/ppermute | solution.py:284
  111.5 1.6 %shard_map.65.refs_1_ = f32[4096,128]{1,0:T(8,128)} custom-call(s32[2]{0:T(128)S(1)} %pad_add_fusion.sources, f32[4096,128]{1,0:T(8,128)S(1)} %copy-done, f32[1024,128]{1,0:T(8,128)S(1)} %collective-permute-done.15.refs_0_, f32[1024,128]{1,0:T(8,128)S(1)} %collective-permute-done.16.refs_1_, ...), custom_call_target="tpu_custom_call", output_to_operand_aliasing={{}: (4, {})} | custom-call | flops 524288 | bytes 1572864 | tf_op jit(solution)/shard_map/pallas_call | solution.py:202
  113.1 0.8 shard_map.66
  (22 shorter events, 3.5 us)
Async XLA Ops:
  2.0 9.4 %all-to-all-start = ((f32[4,16,384]{2,1,0:T(8,128)}), f32[4,16,384]{2,1,0:T(8,128)S(1)}, u32[]{:S(2)}, u32[]{:S(2)}) async-start(f32[4,16,384]{2,1,0:T(8,128)} %shard_map.59), calls=%async_computation | async-start | bytes 196608 | tf_op jit(solution)/shard_map/all_to_all | solution.py:270
  11.4 28.1 %collective-permute-start.6 = (f32[1024,256]{1,0:T(8,128)}, f32[1024,256]{1,0:T(8,128)S(1)}, u32[]{:S(2)}, u32[]{:S(2)}) collective-permute-start(f32[1024,256]{1,0:T(8,128)} %get-tuple-element.29), channel_id=1, source_target_pairs={{0,2},{1,3},{2,0},{3,1},{4,6},{5,7},{6,4},{7,5},{8,10},{9,11},{10,... | collective-permute-start | bytes 3145736 | tf_op jit(solution)/shard_map/ppermute | solution.py:284
  14.7 21.2 %all-to-all-start.1 = ((f32[8,16,768]{2,1,0:T(8,128)}), f32[8,16,768]{2,1,0:T(8,128)S(1)}, u32[]{:S(2)}, u32[]{:S(2)}) async-start(f32[8,16,768]{2,1,0:T(8,128)} %shard_map.60), calls=%async_computation.1 | async-start | bytes 786432 | tf_op jit(solution)/shard_map/all_to_all | solution.py:270
  22.5 35.3 %collective-permute-start.7 = (f32[1024,256]{1,0:T(8,128)}, f32[1024,256]{1,0:T(8,128)}, u32[]{:S(2)}, u32[]{:S(2)}) collective-permute-start(f32[1024,256]{1,0:T(8,128)} %get-tuple-element.30), channel_id=1, source_target_pairs={{0,1},{1,2},{2,3},{3,0},{4,5},{5,6},{6,7},{7,4},{8,9},{9,10},{10,1... | collective-permute-start | bytes 3145736 | tf_op jit(solution)/shard_map/ppermute | solution.py:284
  24.1 35.2 %collective-permute-start.8 = (f32[1024,256]{1,0:T(8,128)}, f32[1024,256]{1,0:T(8,128)}, u32[]{:S(2)}, u32[]{:S(2)}) collective-permute-start(f32[1024,256]{1,0:T(8,128)} %get-tuple-element.31), channel_id=1, source_target_pairs={{0,3},{1,0},{2,1},{3,2},{4,7},{5,4},{6,5},{7,6},{8,11},{9,8},{10,9... | collective-permute-start | bytes 3145736 | tf_op jit(solution)/shard_map/ppermute | solution.py:284
  24.5 4.8 %collective-permute-start = (f32[3,16,256]{2,1,0:T(8,128)S(1)}, f32[3,16,256]{2,1,0:T(8,128)S(1)}, u32[]{:S(2)}, u32[]{:S(2)}) collective-permute-start(f32[3,16,256]{2,1,0:T(8,128)S(1)} %slice.2), channel_id=1, source_target_pairs={{0,192},{4,196},{8,200},{12,204},{16,208},{20,212},{24,216},{28,22... | collective-permute-start | bytes 147464 | tf_op jit(solution)/shard_map/ppermute | solution.py:280
  27.5 5.7 %collective-permute-start.1 = (f32[3,16,256]{2,1,0:T(8,128)S(1)}, f32[3,16,256]{2,1,0:T(8,128)S(1)}, u32[]{:S(2)}, u32[]{:S(2)}) collective-permute-start(f32[3,16,256]{2,1,0:T(8,128)S(1)} %slice.2), channel_id=1, source_target_pairs={{0,128},{4,132},{8,136},{12,140},{16,144},{20,148},{24,152},{28,15... | collective-permute-start | bytes 147464 | tf_op jit(solution)/shard_map/ppermute | solution.py:280
  29.2 5.6 %collective-permute-start.2 = (f32[3,16,256]{2,1,0:T(8,128)S(1)}, f32[3,16,256]{2,1,0:T(8,128)S(1)}, u32[]{:S(2)}, u32[]{:S(2)}) collective-permute-start(f32[3,16,256]{2,1,0:T(8,128)S(1)} %slice.2), channel_id=1, source_target_pairs={{0,64},{4,68},{8,72},{12,76},{16,80},{20,84},{24,88},{28,92},{32,9... | collective-permute-start | bytes 147464 | tf_op jit(solution)/shard_map/ppermute | solution.py:280
  35.9 21.8 %collective-permute-start.3 = (f32[8,16,768]{2,1,0:T(8,128)S(1)}, f32[8,16,768]{2,1,0:T(8,128)}, u32[]{:S(2)}, u32[]{:S(2)}) collective-permute-start(f32[8,16,768]{2,1,0:T(8,128)S(1)} %all-to-all-done.1.refs_0_), channel_id=1, source_target_pairs={{0,192},{4,196},{8,200},{12,204},{16,208},{20,212},{24,216},{28,22... | collective-permute-start | bytes 1179656 | tf_op jit(solution)/shard_map/ppermute | solution.py:280
  38.9 19.3 %collective-permute-start.4 = (f32[8,16,768]{2,1,0:T(8,128)S(1)}, f32[8,16,768]{2,1,0:T(8,128)}, u32[]{:S(2)}, u32[]{:S(2)}) collective-permute-start(f32[8,16,768]{2,1,0:T(8,128)S(1)} %all-to-all-done.1.refs_0_), channel_id=1, source_target_pairs={{0,128},{4,132},{8,136},{12,140},{16,144},{20,148},{24,152},{28,15... | collective-permute-start | bytes 1179656 | tf_op jit(solution)/shard_map/ppermute | solution.py:280
  39.6 18.8 %collective-permute-start.5 = (f32[8,16,768]{2,1,0:T(8,128)S(1)}, f32[8,16,768]{2,1,0:T(8,128)}, u32[]{:S(2)}, u32[]{:S(2)}) collective-permute-start(f32[8,16,768]{2,1,0:T(8,128)S(1)} %all-to-all-done.1.refs_0_), channel_id=1, source_target_pairs={{0,64},{4,68},{8,72},{12,76},{16,80},{20,84},{24,88},{28,92},{32,9... | collective-permute-start | bytes 1179656 | tf_op jit(solution)/shard_map/ppermute | solution.py:280
  42.0 27.7 %all-to-all-start.2 = ((f32[8,6,16,256]{3,2,1,0:T(8,128)}), f32[8,6,16,256]{3,2,1,0:T(8,128)S(1)}, u32[]{:S(2)}, u32[]{:S(2)}) async-start(f32[8,6,16,256]{3,2,1,0:T(8,128)} %shard_map.61), calls=%async_computation.2 | async-start | bytes 1572864 | tf_op jit(solution)/shard_map/all_to_all | solution.py:270
  57.7 2.2 %collective-permute-start.9 = (f32[8,16,768]{2,1,0:T(8,128)S(1)}, f32[8,16,768]{2,1,0:T(8,128)S(1)}, u32[]{:S(2)}, u32[]{:S(2)}) collective-permute-start(f32[8,16,768]{2,1,0:T(8,128)S(1)} %all-to-all-done.1.refs_0_), channel_id=1, source_target_pairs={{0,4},{4,0},{8,12},{12,8},{16,20},{20,16},{24,28},{28,24},{32,36},... | collective-permute-start | bytes 1179656 | tf_op jit(solution)/shard_map/ppermute | solution.py:274
  57.7 2.5 %collective-permute-start.10 = (f32[8,16,768]{2,1,0:T(8,128)}, f32[8,16,768]{2,1,0:T(8,128)S(1)}, u32[]{:S(2)}, u32[]{:S(2)}) collective-permute-start(f32[8,16,768]{2,1,0:T(8,128)} %collective-permute-done.3.refs_1_), channel_id=1, source_target_pairs={{0,4},{4,0},{8,12},{12,8},{16,20},{20,16},{24,28},{28,24},{32,36},... | collective-permute-start | bytes 1179656 | tf_op jit(solution)/shard_map/ppermute | solution.py:274
  58.2 2.5 %collective-permute-start.11 = (f32[8,16,768]{2,1,0:T(8,128)}, f32[8,16,768]{2,1,0:T(8,128)S(1)}, u32[]{:S(2)}, u32[]{:S(2)}) collective-permute-start(f32[8,16,768]{2,1,0:T(8,128)} %collective-permute-done.4.refs_2_), channel_id=1, source_target_pairs={{0,4},{4,0},{8,12},{12,8},{16,20},{20,16},{24,28},{28,24},{32,36},... | collective-permute-start | bytes 1179656 | tf_op jit(solution)/shard_map/ppermute | solution.py:274
  58.3 3.0 %collective-permute-start.12 = (f32[8,16,768]{2,1,0:T(8,128)}, f32[8,16,768]{2,1,0:T(8,128)S(1)}, u32[]{:S(2)}, u32[]{:S(2)}) collective-permute-start(f32[8,16,768]{2,1,0:T(8,128)} %collective-permute-done.5.refs_3_), channel_id=1, source_target_pairs={{0,4},{4,0},{8,12},{12,8},{16,20},{20,16},{24,28},{28,24},{32,36},... | collective-permute-start | bytes 1179656 | tf_op jit(solution)/shard_map/ppermute | solution.py:274
  69.8 2.3 %collective-permute-start.13 = (f32[8,6,16,256]{3,2,1,0:T(8,128)S(1)}, f32[8,6,16,256]{3,2,1,0:T(8,128)S(1)}, u32[]{:S(2)}, u32[]{:S(2)}) collective-permute-start(f32[8,6,16,256]{3,2,1,0:T(8,128)S(1)} %all-to-all-done.2.low_own), channel_id=1, source_target_pairs={{0,4},{4,0},{8,12},{12,8},{16,20},{20,16},{24,28},{28,24},{32,36},... | collective-permute-start | bytes 2359304 | tf_op jit(solution)/shard_map/ppermute | solution.py:274
  72.0 15.9 %copy-start = (f32[4096,128]{1,0:T(8,128)S(1)}, f32[4096,128]{1,0:T(8,128)}, u32[]{:S(2)}) copy-start(f32[4096,128]{1,0:T(8,128)} %rhs.5) | copy-start | bytes 6291460
  83.2 24.9 %collective-permute-start.15 = (f32[1024,128]{1,0:T(8,128)S(1)}, f32[1024,128]{1,0:T(8,128)S(1)}, u32[]{:S(2)}, u32[]{:S(2)}) collective-permute-start(f32[1024,128]{1,0:T(8,128)S(1)} %get-tuple-element.43), channel_id=1, source_target_pairs={{0,1},{1,2},{2,3},{3,0},{4,5},{5,6},{6,7},{7,4},{8,9},{9,10},{10,1... | collective-permute-start | bytes 1572872 | tf_op jit(solution)/shard_map/ppermute | solution.py:284
  85.3 26.1 %collective-permute-start.16 = (f32[1024,128]{1,0:T(8,128)S(1)}, f32[1024,128]{1,0:T(8,128)S(1)}, u32[]{:S(2)}, u32[]{:S(2)}) collective-permute-start(f32[1024,128]{1,0:T(8,128)S(1)} %get-tuple-element.44), channel_id=1, source_target_pairs={{0,3},{1,0},{2,1},{3,2},{4,7},{5,4},{6,5},{7,6},{8,11},{9,8},{10,9... | collective-permute-start | bytes 1572872 | tf_op jit(solution)/shard_map/ppermute | solution.py:284
  85.3 27.7 %collective-permute-start.14 = (f32[1024,128]{1,0:T(8,128)S(1)}, f32[1024,128]{1,0:T(8,128)S(1)}, u32[]{:S(2)}, u32[]{:S(2)}) collective-permute-start(f32[1024,128]{1,0:T(8,128)S(1)} %get-tuple-element.42), channel_id=1, source_target_pairs={{0,2},{1,3},{2,0},{3,1},{4,6},{5,7},{6,4},{7,5},{8,10},{9,11},{10,... | collective-permute-start | bytes 1572872 | tf_op jit(solution)/shard_map/ppermute | solution.py:284
